TPU v7x, 512 devices: a whole 4x4x16 slice. The times are simulated.
512 devices in a mesh: ckpt: 8 (over x, z_hi), unit: 64 (over z_lo, y, core).
Axes of the slice: x: 4, y: 4, z: 16 (z_hi: 2, z_lo: 8; z = z_hi * 8 + z_lo), core: 2. Of those that a mesh axis runs over, the one named last changes fastest.
Arguments:
- train_acts: bfloat16 [8, 4096, 22016], P('ckpt', None, 'unit'), may hold values from -6 to 6
- train_grads: bfloat16 [8, 4096, 8192], P('ckpt', None, 'unit'), may hold values from -6 to 6
- query_acts: bfloat16 [8, 512, 22016], P('ckpt', None, 'unit'), may hold values from -6 to 6
- query_grads: bfloat16 [8, 512, 8192], P('ckpt', None, 'unit'), may hold values from -6 to 6
- query_segment: int32 [512], replicated, may hold values from 0 to 63, never falling along the last dimension, each value on 1 to 16 neighbouring positions
- proj_act: bfloat16 [22016, 64], P('unit'), may hold values from -0.0390625 to 0.0390625
- proj_grad: bfloat16 [8192, 64], P('unit'), may hold values from -0.0625 to 0.0625
- lrates: float32 [8], P('ckpt'), may hold values from 0.001 to 0.01
Outputs:
- scores: float32 [4096, 64], P('unit', 'ckpt')
Inputs may be any that keep to these rules, and one draw needn't show every extreme that they name: `query_segment`: query tokens come grouped by sequence in order; each of the 64 sequences holds 1 to 16 tokens, one exactly 16.
All inputs are finite; a program needn't handle non-finite values.
Results may differ from a plain program's by a relative error of at most 0.0003.
Values may be sent and summed in bfloat16 or wider, within the bound.
A program may use at most 64 MiB of HBM per device.

v0:
```python
import jax
import jax.numpy as jnp
from jax import lax
from jax.sharding import PartitionSpec as P

NQ = 64


def project_rows(act_rows, grad_rows, basis_act, basis_grad):
    part_act = jnp.dot(act_rows, basis_act, preferred_element_type=jnp.float32)
    part_grad = jnp.dot(grad_rows, basis_grad, preferred_element_type=jnp.float32)
    return jnp.concatenate([part_act, part_grad], axis=1)


def body(
    train_acts, train_grads, query_acts, query_grads, query_segment, proj_act, proj_grad, lrates
):
    highest = lax.Precision.HIGHEST
    tok_act = train_acts[0]
    tok_grad = train_grads[0]
    query_act_rows = query_acts[0]
    query_grad_rows = query_grads[0]
    k_act = proj_act.shape[1]
    k_grad = proj_grad.shape[1]
    tok_rows = tok_act.shape[0] // lax.axis_size("unit")
    joined = lax.psum_scatter(
        project_rows(tok_act, tok_grad, proj_act, proj_grad),
        "unit",
        scatter_dimension=0,
        tiled=True,
    )
    train_a = joined[:, :k_act]
    train_g = joined[:, k_act:]
    query_part = project_rows(query_act_rows, query_grad_rows, proj_act, proj_grad)
    query_joined = lax.psum(query_part, "unit")
    query_a = query_joined[:, :k_act]
    query_g = query_joined[:, k_act:]
    onehot = (query_segment[:, None] == jnp.arange(NQ, dtype=jnp.int32)[None, :]).astype(
        jnp.float32
    )
    spread = (onehot[:, :, None] * query_g[:, None, :]).reshape(query_g.shape[0], NQ * k_grad)
    query_basis = jnp.dot(query_a.T, spread, precision=highest)
    middle = jnp.dot(train_a, query_basis, precision=highest).reshape(tok_rows, NQ, k_grad)
    ckpt_score = jnp.sum(middle * train_g[:, None, :], axis=2)
    weighted = lrates[0] * ckpt_score
    return lax.psum_scatter(weighted, "ckpt", scatter_dimension=1, tiled=True)


def solution(mesh):
    placed = (
        P("ckpt", None, "unit"),
        P("ckpt", None, "unit"),
        P("ckpt", None, "unit"),
        P("ckpt", None, "unit"),
        P(),
        P("unit", None),
        P("unit", None),
        P("ckpt"),
    )
    return jax.shard_map(
        body, mesh=mesh, in_specs=placed, out_specs=P("unit", "ckpt"), check_vma=False
    )
```

profile of v0, /device:TPU:1, one launch (start us, length us, event | category | flops | bytes accessed | tf_op | source)
XLA Modules:
  0.0 1317.3 jit_solution(5395536725526717421)
XLA Ops:
  6.5 0.0 copy-start
  6.5 0.0 all-reduce.3.cloned.1.call-start
  6.5 1.3 fusion.4
  7.9 1.1 fusion.8
  8.9 0.7 pad_maximum_fusion.1
  9.7 0.0 all-reduce.3.cloned.1.call-update
  9.7 0.0 copy-start.4
  9.7 0.0 reduce-scatter.4.cloned.1.call-start
  9.8 0.0 copy-done
  9.8 0.0 copy-start.1
  9.8 1.5 fusion
  11.3 0.0 copy-done.4
  11.3 0.0 copy-done.1
  11.3 0.5 fusion.2
  11.8 1.5 pad_maximum_fusion
  13.3 0.0 copy-start.5
  13.3 2.9 copy.14
  16.2 0.0 reduce-scatter.4.cloned.1.call-update
  16.9 1.3 dynamic-slice
  18.8 0.0 copy-done.5
  18.8 778.9 %all-reduce.3.cloned.1.call-done = f32[512,128]{0,1:T(8,128)} async-done(((f32[512,128]{0,1:T(8,128)}), f32[512,128]{0,1:T(8,128)}) %all-reduce.3.cloned.1.call-update) | async-done | bytes 262160 | tf_op jit(solution)/shard_map/psum | solution.py:35
  797.8 0.9 slice.18
  798.7 0.0 copy-start.2
  798.7 1.1 broadcast_multiply_fusion
  799.8 0.0 copy-done.2
  799.8 9.0 fusion.6
  808.8 420.9 %reduce-scatter.4.cloned.1.call-done = f32[64,128]{1,0:T(8,128)} async-done(((f32[4096,128]{1,0:T(8,128)}), f32[64,128]{1,0:T(8,128)}) %reduce-scatter.4.cloned.1.call-update) | async-done | bytes 32784
  1229.7 0.0 copy-start.3
  1229.7 3.2 fusion.11
  1233.0 3.1 reshape.31
  1236.1 0.0 copy-done.3
  1236.1 0.1 slice.19
  1236.2 2.2 multiply_reduce_fusion
  1238.4 0.1 copy.13
  1238.5 71.4 %all-reduce = f32[64,64]{0,1:T(8,128)S(1)} all-reduce(f32[64,64]{0,1:T(8,128)S(1)} %copy.13), channel_id=3, replica_groups=mesh['ckpt'=8,'unit'=64] {'ckpt'}, use_global_device_ids=true, to_apply=%region_3.0.clone | all-reduce | flops 4096 | bytes 32768
  1309.9 0.6 constant_dynamic-slice_fusion
  (2 shorter events, 0.0 us)
Async XLA Ops:
  6.5 3.2 copy-start
  6.5 791.2 %all-reduce.3.cloned.1.call-start = ((), (), s32[]{:S(2)}) async-start(), calls=%async_computation.1 | async-start | bytes 524288 | tf_op jit(solution)/shard_map/psum | solution.py:35
  9.7 1.6 copy-start.4
  9.7 1220.0 %reduce-scatter.4.cloned.1.call-start = ((), (), s32[]{:S(2)}) async-start(), calls=%async_computation.2 | async-start | bytes 2129920
  9.8 1.6 copy-start.1
  13.3 5.5 copy-start.5
  798.7 1.1 copy-start.2
  1229.7 6.4 copy-start.3
Sparse Core Ops, SparseCore 0:
  10.3 787.4 all-reduce.2
  800.8 428.9 reduce-scatter.3
where the time goes:
time: 1320 us
  waiting for transfers between devices  1200 us (91%)
  blocking collectives  71.4 us (5%)
  matrix products  16.7 us (1%)
  between operations  14.8 us (1%)
    psum x1, waiting for transfers between devices, body(): query_joined = lax.psum(query_part, 'unit')  779 us
    unnamed x3, waiting for transfers between devices  421 us
    unnamed x1, blocking collectives  71.4 us
  transfers between devices with their start and end apart: 2, of which 2 were waited for; matrix products, arithmetic and copies ran while one was open for 1% of the time, Pallas kernels for 0%

commit v1 on v0

v1 whole, which is shorter than its diff:
```python
import jax
import jax.numpy as jnp
from jax import lax
from jax.experimental import pallas as pl
from jax.experimental.pallas import tpu as pltpu
from jax.sharding import PartitionSpec as P

MESH = pl.DeviceIdType.MESH
NX, NZ, NY = 4, 8, 4
NQ = 64
ROWS = 64
BLOCK = NY * 2 * ROWS
HALF = 64
QTOK = 512
LANES = 128


def flip(v, bit):
    return v + bit - 2 * bit * lax.rem(lax.div(v, bit), 2)


def kernel(
    ta, tg, qa, qg, seg, pa, pg, lr, out,
    xa, xg, xqa, xqg, xseg, wa, wg, xlr, ins,
    part, c_in, y1_out, y1_in, y2_out, y2_in, acc, z_in,
    qpart, qc_in, qy_out, qy_in, qz_out, qz_in, qall, p_out, p_in, s_out, s_in,
    ssem, rsem,
):
    c = lax.axis_index("ckpt")
    u = lax.axis_index("unit")
    x, zh = lax.div(c, 2), lax.rem(c, 2)
    z, y, k = lax.div(u, 8), lax.rem(lax.div(u, 2), 4), lax.rem(u, 2)

    def at(x_, zh_, z_, y_, k_):
        return (x_ * 2 + zh_, (z_ * NY + y_) * 2 + k_)

    def p1(v):
        return (1 - k) * flip(v, 1) + k * (3 - v)

    def p2(v):
        return (1 - k) * (3 - v) + k * flip(v, 1)

    ya, yb = p1(y), p2(y)
    sib = at(x, zh, z, y, 1 - k)
    y_peers = [at(x, zh, z, lax.rem(y + d, NY), k) for d in range(1, NY)]
    z_peers = [at(x, zh, lax.rem(z + d, NZ), y, k) for d in range(1, NZ)]
    home = flip(z, 4)
    c_peers = [
        at(lax.rem(x + d, NX), lax.rem(zh + e, 2), home, y, k)
        for d in range(NX)
        for e in range(2)
    ]
    partners = [sib] + y_peers + z_peers + c_peers[1:]

    loads = {}

    def load(name, src, dst):
        cp = pltpu.make_async_copy(src, dst, ins.at[len(loads)])
        cp.start()
        loads[name] = cp

    load("qa", qa, xqa)
    load("qg", qg, xqg)
    load("pa", pa, wa)
    load("pg", pg, wg)

    def by_bits(m):
        v = z
        for b in (1, 2, 4):
            if m & b:
                v = flip(v, b)
        return v

    for m in range(NZ - 1, -1, -1):
        cols = pl.ds(pl.multiple_of(by_bits(m ^ 4) * BLOCK, BLOCK), BLOCK)
        load(f"ta{m}", ta.at[:, cols], xa.at[m])
        load(f"tg{m}", tg.at[cols], xg.at[m])
    load("seg", seg, xseg)
    load("lr", lr, xlr)

    barrier = pltpu.get_barrier_semaphore()
    for p in partners:
        pl.semaphore_signal(barrier, inc=1, device_id=p, device_id_type=MESH)

    sent = []

    def send(src, dst, to):
        i = len(sent)
        cp = pltpu.make_async_remote_copy(
            src_ref=src, dst_ref=dst, send_sem=ssem.at[i], recv_sem=rsem.at[i],
            device_id=to, device_id_type=MESH,
        )
        cp.start()
        sent.append(cp)
        return cp

    def project(dst, acts, grads):
        a = jnp.dot(wa[...], acts, preferred_element_type=jnp.float32)
        g = lax.dot_general(
            wg[...], grads, (((1,), (1,)), ((), ())), preferred_element_type=jnp.float32
        )
        for j in range(NY):
            dst[0, j] = a[:, j * LANES : (j + 1) * LANES]
            dst[1, j] = g[:, j * LANES : (j + 1) * LANES]

    for n in ("pa", "pg", "qa", "qg"):
        loads[n].wait()
    project(qpart, xqa[...], xqg[...])
    pl.semaphore_wait(barrier, len(partners))
    qc = send(qpart.at[1 - k], qc_in, sib)

    c_cp, y1_cp, y2_cp, z_cp = {}, {}, {}, {}

    def stage_c(m):
        loads[f"ta{m}"].wait()
        loads[f"tg{m}"].wait()
        project(part.at[m], xa[m], xg[m])
        c_cp[m] = send(part.at[m, 1 - k], c_in.at[m], sib)

    def stage_y1(m):
        c_cp[m].wait_recv()
        y1_out[m, 0] = part[m, k, ya] + c_in[m, ya]
        yab = p2(ya)
        y1_out[m, 1] = part[m, k, yab] + c_in[m, yab]
        y1_cp[m] = send(y1_out.at[m], y1_in.at[m], at(x, zh, z, ya, k))

    def stage_y2(m):
        y1_cp[m].wait_recv()
        y2_out[m] = part[m, k, yb] + c_in[m, yb] + y1_in[m, 1]
        y2_cp[m] = send(y2_out.at[m], y2_in.at[m], at(x, zh, z, yb, k))
        acc[m] = part[m, k, y] + c_in[m, y] + y1_in[m, 0]

    def stage_z1(m):
        y2_cp[m].wait_recv()
        acc[m] = acc[m] + y2_in[m]
        if m & 1:
            z_cp[m] = send(acc.at[m], z_in.at[m], at(x, zh, flip(z, 1), y, k))

    def stage_z2(m):
        z_cp[m + 1].wait_recv()
        acc[m] = acc[m] + z_in[m + 1]
        if m & 2:
            z_cp[m] = send(acc.at[m], z_in.at[m], at(x, zh, flip(z, 2), y, k))

    def stage_z3(m):
        z_cp[m + 2].wait_recv()
        acc[m] = acc[m] + z_in[m + 2]
        if m & 4:
            z_cp[m] = send(acc.at[m], z_in.at[m], at(x, zh, flip(z, 4), y, k))

    stage_c(7)
    stage_c(6)
    qc.wait_recv()
    for j in range(NY):
        qy_out[j] = qpart[k, j] + qc_in[j]
    qy = []
    for d in range(1, NY):
        qy.append(send(qy_out.at[lax.rem(y + d, NY)], qy_in.at[d - 1], y_peers[d - 1]))
    stage_c(5)
    stage_c(4)
    stage_y1(7)
    stage_y1(6)
    stage_c(3)
    stage_c(2)
    for cp in qy:
        cp.wait_recv()
    qz_out[...] = (qy_out[y] + qy_in[0] + qy_in[1] + qy_in[2]).reshape(qz_out.shape)
    qz = []
    for d in range(1, NZ):
        qz.append(send(qz_out.at[lax.rem(z + d, NZ)], qz_in.at[d - 1], z_peers[d - 1]))
    stage_y1(5)
    stage_y1(4)
    stage_c(1)
    stage_c(0)
    stage_y1(3)
    stage_y1(2)
    stage_y2(7)
    stage_y2(6)
    stage_y1(1)
    stage_y1(0)
    stage_y2(5)
    stage_y2(4)
    stage_z1(7)
    stage_z1(6)
    for cp in qz:
        cp.wait_recv()
    total = qz_out[z]
    for d in range(NZ - 1):
        total = total + qz_in[d]
    qall[y, z] = total
    mine = qall.at[y, z]
    qz = [send(mine, mine, p) for p in z_peers]
    stage_y2(3)
    stage_y2(2)
    stage_z1(5)
    stage_z1(4)
    stage_z2(6)
    stage_y2(1)
    stage_y2(0)
    stage_z2(4)
    stage_z1(3)
    stage_z1(2)
    stage_z3(4)
    stage_z1(1)
    stage_z1(0)
    stage_z2(2)
    for cp in qz:
        cp.wait_recv()
    line = qall.at[y]
    qy = [send(line, line, p) for p in y_peers]
    stage_z2(0)
    stage_z3(0)
    loads["seg"].wait()
    loads["lr"].wait()
    onehot = (
        lax.broadcasted_iota(jnp.int32, (NQ, QTOK), 0) == xseg[...]
    ).astype(jnp.float32)
    z_cp[4].wait_recv()
    tok = (acc[0] + z_in[4]).T
    for cp in qy:
        cp.wait_recv()
    for j in range(NY):
        match = jnp.dot(
            tok, qall[j].reshape(HALF, LANES),
            precision=lax.Precision.HIGHEST, preferred_element_type=jnp.float32,
        )
        p_out[:, j] = match.reshape(2, ROWS, LANES)
    pc = send(p_out.at[1 - k], p_in, sib)
    pc.wait_recv()
    score = jnp.zeros((NQ, LANES), jnp.float32)
    for j in range(NY):
        prod = p_out[k, j] * p_in[j]
        score += lax.dot_general(
            onehot[:, j * LANES : (j + 1) * LANES],
            jnp.concatenate([prod, prod], axis=0),
            (((1,), (1,)), ((), ())),
            precision=lax.Precision.HIGHEST, preferred_element_type=jnp.float32,
        )
    s_out[...] = (xlr[0] * score).reshape(s_out.shape)
    fin = []
    for i, p in enumerate(c_peers):
        fin.append(send(s_out.at[p[0]], s_in.at[i], p))
    for cp in fin:
        cp.wait_recv()
    total = s_in[0]
    for i in range(1, len(c_peers)):
        total = total + s_in[i]
    out[...] = total[:, :ROWS]
    for cp in sent:
        cp.wait_send()


def body(
    train_acts, train_grads, query_acts, query_grads, query_segment, proj_act, proj_grad, lrates
):
    ff, d = train_acts.shape[2], train_grads.shape[2]
    f32, bf16 = jnp.float32, jnp.bfloat16
    vmem = pltpu.VMEM
    nsend = 80
    hbm = pl.BlockSpec(memory_space=pltpu.HBM)
    res = pl.pallas_call(
        kernel,
        out_shape=jax.ShapeDtypeStruct((8, ROWS), f32),
        in_specs=[hbm] * 8,
        out_specs=pl.BlockSpec(memory_space=pltpu.VMEM),
        scratch_shapes=[
            vmem((NZ, ff, BLOCK), bf16),
            vmem((NZ, BLOCK, d), bf16),
            vmem((ff, QTOK), bf16),
            vmem((QTOK, d), bf16),
            vmem((1, QTOK), jnp.int32),
            vmem((HALF, ff), bf16),
            vmem((HALF, d), bf16),
            pltpu.SMEM((1,), f32),
            pltpu.SemaphoreType.DMA((2 * NZ + 6,)),
            vmem((NZ, 2, NY, HALF, LANES), f32),
            vmem((NZ, NY, HALF, LANES), f32),
            vmem((NZ, 2, HALF, LANES), f32),
            vmem((NZ, 2, HALF, LANES), f32),
            vmem((NZ, HALF, LANES), f32),
            vmem((NZ, HALF, LANES), f32),
            vmem((NZ, HALF, LANES), f32),
            vmem((NZ, HALF, LANES), f32),
            vmem((2, NY, HALF, LANES), f32),
            vmem((NY, HALF, LANES), f32),
            vmem((NY, HALF, LANES), f32),
            vmem((NY - 1, HALF, LANES), f32),
            vmem((NZ, 8, LANES), f32),
            vmem((NZ - 1, 8, LANES), f32),
            vmem((NY, NZ, 8, LANES), f32),
            vmem((2, NY, ROWS, LANES), f32),
            vmem((NY, ROWS, LANES), f32),
            vmem((8, 8, LANES), f32),
            vmem((8, 8, LANES), f32),
            pltpu.SemaphoreType.DMA((nsend,)),
            pltpu.SemaphoreType.DMA((nsend,)),
        ],
        compiler_params=pltpu.CompilerParams(
            collective_id=0, has_side_effects=True, vmem_limit_bytes=60 << 20
        ),
        name="tracin",
    )(
        train_acts[0].T,
        train_grads[0],
        query_acts[0].T,
        query_grads[0],
        query_segment.reshape(1, QTOK),
        proj_act.T,
        proj_grad.T,
        lrates,
    )
    return res.T


def solution(mesh):
    placed = (
        P("ckpt", None, "unit"),
        P("ckpt", None, "unit"),
        P("ckpt", None, "unit"),
        P("ckpt", None, "unit"),
        P(),
        P("unit", None),
        P("unit", None),
        P("ckpt"),
    )
    return jax.shard_map(
        body, mesh=mesh, in_specs=placed, out_specs=P("unit", "ckpt"), check_vma=False
    )
```

time: 1320 us -> 52.8 us (0.04)
  waiting for transfers between devices: 1200 us -> 0 us
  blocking collectives: 71.4 us -> 0 us
  Pallas kernels: 0 us -> 50.7 us
  matrix products: 16.7 us -> 0 us
  between operations: 14.8 us -> 0.66 us
    psum x1 -> x0, waiting for transfers between devices: 779 us -> none  [body(): query_joined = lax.psum(query_part, 'unit')]
    unnamed x3 -> x0, waiting for transfers between devices: 421 us -> none
    unnamed x1 -> x0, blocking collectives: 71.4 us -> none
    pallas_call x0 -> x1, Pallas kernels: none -> 50.7 us  [body(): pl.pallas_call(kernel, out_shape=jax.ShapeDtypeStruct((8, ROWS), f32), in...]
    dot_general x6 -> x0, matrix products: 16.7 us -> none  [the longest x1 9.03 us: body(): query_basis = jnp.dot(query_a.T, spread, precision=highest)]
  transfers between devices with their start and end apart: 2 -> 0, of which waited for: 2 -> 0; matrix products, arithmetic and copies ran while one was open for 1% -> 0% of each run, Pallas kernels for 0% -> 0%
where the time goes in v1:
time: 52.8 us; the launch traced here: 52.7 us
  Pallas kernels  50.7 us (96%)
  local copies, waits for them, and re-layouts  1.28 us (2%)
  between operations  0.66 us (1%)
    pallas_call x1, Pallas kernels, body(): pl.pallas_call(kernel, out_shape=jax.ShapeDtypeStruct((8, ROWS), f32), in...  50.7 us
    unnamed x1, local copies, waits for them, and re-layouts  1.28 us

profile of v1, /device:TPU:1, one launch (start us, length us, event | category | flops | bytes accessed | tf_op | source)
XLA Modules:
  0.0 52.7 jit_solution(17108404774682422023)
XLA Ops:
  0.7 50.7 %tracin.1 = f32[8,64]{1,0:T(8,128)} custom-call(bf16[344,4096]{1,0:T(8,128)(2,1)} %bitcast.12, bf16[4096,128]{1,0:T(8,128)(2,1)} %bitcast.13, bf16[344,512]{1,0:T(8,128)(2,1)} %bitcast.14, bf16[512,128]{1,0:T(8,128)(2,1)} %bitcast.15, s32[1,512]{1,0:T(1,128)} %bitcast.19, bf16[64,344]{1,0:T(8,128)(2,1)} %bitcast.16, bf16[64,128]{1,0:T(8,128)(2,1)} %bitcast.17, ...), custom_call_target="tpu_custom_call" | custom-call | tf_op jit(solution)/shard_map/tracin/pallas_call | solution.py:261
  51.4 1.3 %copy.11 = f32[64,8]{0,1:T(8,128)} copy(f32[64,8]{0,1:T(8,128)} %bitcast.18) | data formatting | bytes 4096

commit v2 on v1

v2 whole, which is shorter than its diff:
```python
import jax
import jax.numpy as jnp
from jax import lax
from jax.experimental import pallas as pl
from jax.experimental.pallas import tpu as pltpu
from jax.sharding import PartitionSpec as P

MESH = pl.DeviceIdType.MESH
NX, NZ, NY = 4, 8, 4
NQ = 64
ROWS = 64
BLOCK = NY * 2 * ROWS
NP = NZ // 2
HALF = 64
QH = HALF // 2
SCALE = 16
QTOK = 512
LANES = 128
TOP = 32760.0


def flip(v, bit):
    return v + bit - 2 * bit * lax.rem(lax.div(v, bit), 2)


def put(ref, groups):
    at, logs = 0, []
    for blocks in groups:
        top = jnp.max(jnp.abs(blocks[0]), axis=0, keepdims=True)
        for v in blocks[1:]:
            top = jnp.maximum(top, jnp.max(jnp.abs(v), axis=0, keepdims=True))
        log = jnp.ceil(jnp.log2(jnp.maximum(top, 1e-30)) * 256.0)
        unit = jnp.exp2(log * (-1.0 / 256.0)) * TOP
        for v in blocks:
            n = v.shape[0]
            ref[at : at + n] = jnp.round(v * unit).astype(jnp.int32).astype(jnp.int16)
            at += n
        logs.append(jnp.broadcast_to(log.astype(jnp.int32), (SCALE // len(groups), LANES)))
    ref[at : at + SCALE] = jnp.concatenate(logs, axis=0).astype(jnp.int16)


def get(ref, groups, rows):
    n = ref.shape[0] - SCALE
    logs = ref[n:].astype(jnp.int32).astype(jnp.float32)
    step = SCALE // groups
    found = []
    for i in range(groups):
        unit = jnp.exp2(logs[i * step : i * step + 1] * (1.0 / 256.0)) * (1.0 / TOP)
        start, end = i * n // groups, (i + 1) * n // groups
        found.append([
            ref[r : r + rows].astype(jnp.int32).astype(jnp.float32) * unit
            for r in range(start, end, rows)
        ])
    return found


def kernel(
    ta, tg, qa, qg, seg, pa, pg, lr, out,
    xa, xg, xqa, xqg, xseg, wa, wg, xlr, ins,
    part, c_in, y1_out, y1_in, y2_out, y2_in, z_out, z_in, keep, acc,
    qpart, qc_in, qy_own, qy_out, qy_in, qz_own, qz_out, qz_in, qall, p_out, p_in, s_out, s_in,
    ssem, rsem,
):
    c = lax.axis_index("ckpt")
    u = lax.axis_index("unit")
    x, zh = lax.div(c, 2), lax.rem(c, 2)
    z, y, k = lax.div(u, 8), lax.rem(lax.div(u, 2), 4), lax.rem(u, 2)

    def at(x_, zh_, z_, y_, k_):
        return (x_ * 2 + zh_, (z_ * NY + y_) * 2 + k_)

    def p1(v):
        return (1 - k) * flip(v, 1) + k * (3 - v)

    def p2(v):
        return (1 - k) * (3 - v) + k * flip(v, 1)

    ya, yb = p1(y), p2(y)
    yab = p2(ya)
    sib = at(x, zh, z, y, 1 - k)
    y_peers = [at(x, zh, z, lax.rem(y + d, NY), k) for d in range(1, NY)]
    z_peers = [at(x, zh, lax.rem(z + d, NZ), y, k) for d in range(1, NZ)]
    home = flip(z, 4)
    c_peers = [
        at(lax.rem(x + d, NX), lax.rem(zh + e, 2), home, y, k)
        for d in range(NX)
        for e in range(2)
    ]
    partners = [sib] + y_peers + z_peers + c_peers[1:]

    barrier = pltpu.get_barrier_semaphore()
    for p in partners:
        pl.semaphore_signal(barrier, inc=1, device_id=p, device_id_type=MESH)

    loads = {}

    def load(name, src, dst):
        cp = pltpu.make_async_copy(src, dst, ins.at[len(loads)])
        cp.start()
        loads[name] = cp

    load("qa", qa, xqa)
    load("qg", qg, xqg)
    load("pa", pa, wa)
    load("pg", pg, wg)
    zp = lax.div(z, 2)
    for w in range(NP - 1, -1, -1):
        b = flip(zp, 2)
        for bit in (1, 2):
            b = flip(b, bit) if w & bit else b
        cols = pl.ds(pl.multiple_of(b * (2 * BLOCK), 2 * BLOCK), 2 * BLOCK)
        load(f"ta{w}", ta.at[:, cols], xa.at[w])
        load(f"tg{w}", tg.at[cols], xg.at[w])
    load("seg", seg, xseg)
    load("lr", lr, xlr)

    sems = [0]
    sent = []

    def copy_to(src, dst, to, i):
        return pltpu.make_async_remote_copy(
            src_ref=src, dst_ref=dst, send_sem=ssem.at[i], recv_sem=rsem.at[i],
            device_id=to, device_id_type=MESH,
        )

    def send(src, dst, to):
        cp = copy_to(src, dst, to, sems[0])
        sems[0] += 1
        cp.start()
        sent.append(cp)
        return cp

    def project(acts, grads, store):
        a = jnp.dot(wa[...], acts, preferred_element_type=jnp.float32)
        g = lax.dot_general(
            wg[...], grads, (((1,), (1,)), ((), ())), preferred_element_type=jnp.float32
        )
        for j in range(a.shape[1] // LANES):
            store(0, j, a[:, j * LANES : (j + 1) * LANES])
            store(1, j, g[:, j * LANES : (j + 1) * LANES])

    def project_query():
        for n in ("pa", "pg", "qa", "qg"):
            loads[n].wait()

        def store(h, j, v):
            qpart[h, j] = v

        project(xqa[...], xqg[...], store)

    def project_pair(w):
        loads[f"ta{w}"].wait()
        loads[f"tg{w}"].wait()

        def store(h, j, v):
            part[w, h, j // NY, j % NY] = v

        project(xa[w], xg[w], store)

    cp = {}

    def send_c(w):
        cp["c", w] = send(part.at[w, 1 - k], c_in.at[w], sib)

    def own(w, i, v):
        return part[w, k, i, v] + c_in[w, i, v]

    def stage_y1(w):
        cp["c", w].wait_recv()
        put(y1_out.at[w], [[own(w, i, ya), own(w, i, yab)] for i in range(2)])
        cp["y1", w] = send(y1_out.at[w], y1_in.at[w], at(x, zh, z, ya, k))

    def stage_y2(w):
        cp["y1", w].wait_recv()
        got = get(y1_in.at[w], 2, HALF)
        put(y2_out.at[w], [[own(w, i, yb) + got[i][1]] for i in range(2)])
        cp["y2", w] = send(y2_out.at[w], y2_in.at[w], at(x, zh, z, yb, k))
        for i in range(2):
            keep[w, i] = own(w, i, y) + got[i][0]

    def stage_z1(w):
        cp["y2", w].wait_recv()
        got = get(y2_in.at[w], 2, HALF)
        for i in range(2):
            keep[w, i] = keep[w, i] + got[i][0]
        mine = lax.rem(z, 2)
        put(z_out.at[w, 0], [[keep[w, 1 - mine]]])
        cp["z1", w] = send(z_out.at[w, 0], z_in.at[w, 0], at(x, zh, flip(z, 1), y, k))
        acc[w] = keep[w, mine]

    def stage_z2(w):
        cp["z1", w].wait_recv()
        v = acc[w] + get(z_in.at[w, 0], 1, HALF)[0][0]
        if w % 2:
            put(z_out.at[w, 1], [[v]])
            cp["z2", w] = send(z_out.at[w, 1], z_in.at[w, 1], at(x, zh, flip(z, 2), y, k))
        else:
            acc[w] = v

    def stage_z3():
        cp["z2", 3].wait_recv()
        put(z_out.at[2, 1], [[acc[2] + get(z_in.at[3, 1], 1, HALF)[0][0]]])
        cp["z3"] = send(z_out.at[2, 1], z_in.at[2, 1], at(x, zh, flip(z, 4), y, k))

    project_query()
    project_pair(3)
    pl.semaphore_wait(barrier, len(partners))
    qc = send(qpart.at[1 - k], qc_in, sib)
    send_c(3)
    project_pair(2)
    send_c(2)
    qc.wait_recv()
    for j in range(NY):
        v = qpart[k, j] + qc_in[j]
        qy_own[j] = v
        put(qy_out.at[j], [[v]])
    qy = [
        send(qy_out.at[lax.rem(y + d, NY)], qy_in.at[d - 1], y_peers[d - 1])
        for d in range(1, NY)
    ]
    stage_y1(3)
    project_pair(1)
    send_c(1)
    stage_y1(2)
    project_pair(0)
    send_c(0)
    stage_y1(1)
    stage_y1(0)
    for p in qy:
        p.wait_recv()
    v = qy_own[y]
    for d in range(NY - 1):
        v = v + get(qy_in.at[d], 1, HALF)[0][0]
    first_z, first_b = sems[0], sems[0] + NZ
    sems[0] += 2 * NZ + 2
    middle = (NZ // 2 - 1, NZ // 2)
    for h in range(2):
        qz_own[h] = v[h * QH : (h + 1) * QH]
        put(qz_out.at[h], [[v[h * QH : (h + 1) * QH]]])

    def to_middle(h):
        d = lax.rem(z - middle[h] + NZ, NZ)
        return pltpu.make_async_remote_copy(
            src_ref=qz_out.at[h], dst_ref=qz_in.at[d], send_sem=ssem.at[first_z + h],
            recv_sem=rsem.at[first_z + d], device_id=at(x, zh, middle[h], y, k),
            device_id_type=MESH,
        )

    for h in range(2):

        @pl.when(z != middle[h])
        def _():
            to_middle(h).start()

    is_middle = jnp.logical_or(z == middle[0], z == middle[1])
    my_h = 1 - lax.rem(z, 2)

    def from_middle(d):
        place = qall.at[y, my_h]
        return pltpu.make_async_remote_copy(
            src_ref=place, dst_ref=place, send_sem=ssem.at[first_b + 1 + d],
            recv_sem=rsem.at[first_b + my_h], device_id=z_peers[d - 1], device_id_type=MESH,
        )

    def middle_sum():
        @pl.when(is_middle)
        def _():
            total = qz_own[my_h]
            for d in range(1, NZ):
                copy_to(qz_out.at[0], qz_in.at[d], sib, first_z + d).wait_recv()
            for d in range(1, NZ):
                total = total + get(qz_in.at[d], 1, QH)[0][0]
            put(qall.at[y, my_h], [[total]])
            for d in range(1, NZ):
                from_middle(d).start()

    stage_y2(3)
    stage_y2(2)
    stage_y2(1)
    stage_y2(0)
    stage_z1(3)
    stage_z1(2)
    middle_sum()
    stage_z2(3)
    stage_z1(1)
    stage_z2(2)
    stage_z1(0)
    stage_z3()
    stage_z2(1)
    stage_z2(0)
    loads["seg"].wait()
    loads["lr"].wait()
    onehot = jnp.where(
        lax.broadcasted_iota(jnp.int32, (NQ, QTOK), 0) == xseg[...], 1.0, 0.0
    ).astype(jnp.bfloat16)
    for h in range(2):

        @pl.when(z != middle[h])
        def _():
            copy_to(qall.at[y, h], qall.at[y, h], sib, first_b + h).wait_recv()

    line = qall.at[y]
    qy = [send(line, line, p) for p in y_peers]
    cp["z2", 1].wait_recv()
    v = acc[0] + get(z_in.at[1, 1], 1, HALF)[0][0]
    cp["z3"].wait_recv()
    tok = (v + get(z_in.at[2, 1], 1, HALF)[0][0]).T
    for p in qy:
        p.wait_recv()
    for j in range(NY):
        feats = jnp.concatenate([get(qall.at[j, h], 1, QH)[0][0] for h in range(2)], axis=0)
        match = jnp.dot(
            tok, feats, precision=lax.Precision.HIGHEST, preferred_element_type=jnp.float32
        )
        p_out[:, j] = match.reshape(2, ROWS, LANES)
    pc = send(p_out.at[1 - k], p_in, sib)
    pc.wait_recv()
    score = jnp.zeros((NQ, LANES), jnp.float32)
    for j in range(NY):
        prod = p_out[k, j] * p_in[j]
        high = prod.astype(jnp.bfloat16)
        rest = (prod - high.astype(jnp.float32)).astype(jnp.bfloat16)
        score += lax.dot_general(
            onehot[:, j * LANES : (j + 1) * LANES],
            jnp.concatenate([high, rest], axis=0),
            (((1,), (1,)), ((), ())), preferred_element_type=jnp.float32,
        )
    score = xlr[0] * (score + pltpu.roll(score, ROWS, 1))
    s_out[...] = score.reshape(s_out.shape)
    fin = []
    for i, p in enumerate(c_peers):
        fin.append(send(s_out.at[p[0]], s_in.at[i], p))
    for p in fin:
        p.wait_recv()
    total = s_in[0]
    for i in range(1, len(c_peers)):
        total = total + s_in[i]
    out[...] = total[:, :ROWS]
    for p in sent:
        p.wait_send()
    for h in range(2):

        @pl.when(z != middle[h])
        def _():
            to_middle(h).wait_send()

    @pl.when(is_middle)
    def _():
        for d in range(1, NZ):
            from_middle(d).wait_send()


def body(
    train_acts, train_grads, query_acts, query_grads, query_segment, proj_act, proj_grad, lrates
):
    ff, d = train_acts.shape[2], train_grads.shape[2]
    f32, bf16, i16 = jnp.float32, jnp.bfloat16, jnp.int16
    vmem = pltpu.VMEM
    nsem = 80
    hbm = pl.BlockSpec(memory_space=pltpu.HBM)
    res = pl.pallas_call(
        kernel,
        out_shape=jax.ShapeDtypeStruct((8, ROWS), f32),
        in_specs=[hbm] * 8,
        out_specs=pl.BlockSpec(memory_space=pltpu.VMEM),
        scratch_shapes=[
            vmem((NP, ff, 2 * BLOCK), bf16),
            vmem((NP, 2 * BLOCK, d), bf16),
            vmem((ff, QTOK), bf16),
            vmem((QTOK, d), bf16),
            vmem((1, QTOK), jnp.int32),
            vmem((HALF, ff), bf16),
            vmem((HALF, d), bf16),
            pltpu.SMEM((1,), f32),
            pltpu.SemaphoreType.DMA((2 * NP + 6,)),
            vmem((NP, 2, 2, NY, HALF, LANES), f32),
            vmem((NP, 2, NY, HALF, LANES), f32),
            vmem((NP, 4 * HALF + SCALE, LANES), i16),
            vmem((NP, 4 * HALF + SCALE, LANES), i16),
            vmem((NP, 2 * HALF + SCALE, LANES), i16),
            vmem((NP, 2 * HALF + SCALE, LANES), i16),
            vmem((NP, 2, HALF + SCALE, LANES), i16),
            vmem((NP, 2, HALF + SCALE, LANES), i16),
            vmem((NP, 2, HALF, LANES), f32),
            vmem((NP, HALF, LANES), f32),
            vmem((2, NY, HALF, LANES), f32),
            vmem((NY, HALF, LANES), f32),
            vmem((NY, HALF, LANES), f32),
            vmem((NY, HALF + SCALE, LANES), i16),
            vmem((NY - 1, HALF + SCALE, LANES), i16),
            vmem((2, QH, LANES), f32),
            vmem((2, QH + SCALE, LANES), i16),
            vmem((NZ, QH + SCALE, LANES), i16),
            vmem((NY, 2, QH + SCALE, LANES), i16),
            vmem((2, NY, ROWS, LANES), f32),
            vmem((NY, ROWS, LANES), f32),
            vmem((8, 8, LANES), f32),
            vmem((8, 8, LANES), f32),
            pltpu.SemaphoreType.DMA((nsem,)),
            pltpu.SemaphoreType.DMA((nsem,)),
        ],
        compiler_params=pltpu.CompilerParams(
            collective_id=0, has_side_effects=True, vmem_limit_bytes=60 << 20
        ),
        name="tracin",
    )(
        train_acts[0].T,
        train_grads[0],
        query_acts[0].T,
        query_grads[0],
        query_segment.reshape(1, QTOK),
        proj_act.T,
        proj_grad.T,
        lrates,
    )
    return res.T


def solution(mesh):
    placed = (
        P("ckpt", None, "unit"),
        P("ckpt", None, "unit"),
        P("ckpt", None, "unit"),
        P("ckpt", None, "unit"),
        P(),
        P("unit", None),
        P("unit", None),
        P("ckpt"),
    )
    return jax.shard_map(
        body, mesh=mesh, in_specs=placed, out_specs=P("unit", "ckpt"), check_vma=False
    )
```

time: 52.8 us -> 48.1 us (0.911)
  Pallas kernels: 50.7 us -> 46 us
    pallas_call x1, Pallas kernels: 50.7 us -> 46 us  [body(): pl.pallas_call(kernel, out_shape=jax.ShapeDtypeStruct((8, ROWS), f32), in...]
where the time goes in v2:
time: 48.1 us; the launch traced here: 47.9 us
  Pallas kernels  46 us (96%)
  local copies, waits for them, and re-layouts  1.28 us (3%)
  between operations  0.66 us (1%)
    pallas_call x1, Pallas kernels, body(): pl.pallas_call(kernel, out_shape=jax.ShapeDtypeStruct((8, ROWS), f32), in...  46 us
    unnamed x1, local copies, waits for them, and re-layouts  1.28 us

profile of v2, /device:TPU:1, one launch (start us, length us, event | category | flops | bytes accessed | tf_op | source)
XLA Modules:
  0.0 47.9 jit_solution(8559712715189614735)
XLA Ops:
  0.7 46.0 %tracin.1 = f32[8,64]{1,0:T(8,128)} custom-call(bf16[344,4096]{1,0:T(8,128)(2,1)} %bitcast.12, bf16[4096,128]{1,0:T(8,128)(2,1)} %bitcast.13, bf16[344,512]{1,0:T(8,128)(2,1)} %bitcast.14, bf16[512,128]{1,0:T(8,128)(2,1)} %bitcast.15, s32[1,512]{1,0:T(1,128)} %bitcast.19, bf16[64,344]{1,0:T(8,128)(2,1)} %bitcast.16, bf16[64,128]{1,0:T(8,128)(2,1)} %bitcast.17, ...), custom_call_target="tpu_custom_call" | custom-call | tf_op jit(solution)/shard_map/tracin/pallas_call | solution.py:361
  46.6 1.3 %copy.11 = f32[64,8]{0,1:T(8,128)} copy(f32[64,8]{0,1:T(8,128)} %bitcast.18) | data formatting | bytes 4096

commit v3 on v2

v3 whole, which is shorter than its diff:
```python
import jax
import jax.numpy as jnp
from jax import lax
from jax.experimental import pallas as pl
from jax.experimental.pallas import tpu as pltpu
from jax.sharding import PartitionSpec as P

MESH = pl.DeviceIdType.MESH
NX, NZ, NY = 4, 8, 4
NQ = 64
ROWS = 64
BLOCK = NY * 2 * ROWS
NP = NZ // 2
HALF = 64
QH = HALF // 2
QTOK = 512
LANES = 128
TOP = 32760.0


def flip(v, bit):
    return v + bit - 2 * bit * lax.rem(lax.div(v, bit), 2)


def put(ref, groups):
    at, logs = 0, []
    for blocks in groups:
        top = jnp.max(jnp.abs(blocks[0]), axis=0, keepdims=True)
        for v in blocks[1:]:
            top = jnp.maximum(top, jnp.max(jnp.abs(v), axis=0, keepdims=True))
        log = jnp.ceil(jnp.log2(jnp.maximum(top, 1e-30)) * 256.0)
        unit = jnp.exp2(log * (-1.0 / 256.0)) * TOP
        for v in blocks:
            q = jnp.round(v * unit).astype(jnp.int32)
            n = v.shape[0] // 2
            ref[at : at + n] = (q[n:] << 16) | (q[:n] & 0xFFFF)
            at += n
        logs.append(log.astype(jnp.int32))
    for log in logs:
        ref[at : at + 1] = log
        at += 1


def get(ref, groups, rows):
    n, half = ref.shape[0] - groups, rows // 2
    found = []
    for i in range(groups):
        log = ref[n + i : n + i + 1].astype(jnp.float32)
        unit = jnp.exp2(log * (1.0 / 256.0)) * (1.0 / TOP)
        blocks = []
        for r in range(i * n // groups, (i + 1) * n // groups, half):
            v = ref[r : r + half]
            both = jnp.concatenate([(v << 16) >> 16, v >> 16], axis=0)
            blocks.append(both.astype(jnp.float32) * unit)
        found.append(blocks)
    return found


def kernel(
    ta, tg, qa, qg, seg, pa, pg, lr, out,
    xa, xg, xqa, xqg, xseg, wa, wg, xlr, ins,
    part, c_in, y1_out, y1_in, y2_out, y2_in, z_out, z_in, f_out, f_in, keep,
    qpart, qc_in, qy_own, qy_out, qy_in, qz_own, qz_out, qz_in, qall, p_out, p_in, s_out, s_in,
    ssem, rsem, z_sem, x_sem,
):
    c = lax.axis_index("ckpt")
    u = lax.axis_index("unit")
    x, zh = lax.div(c, 2), lax.rem(c, 2)
    z, y, k = lax.div(u, 8), lax.rem(lax.div(u, 2), 4), lax.rem(u, 2)

    def at(x_, zh_, z_, y_, k_):
        return (x_ * 2 + zh_, (z_ * NY + y_) * 2 + k_)

    def p1(v):
        return k * flip(v, 1) + (1 - k) * (3 - v)

    def p2(v):
        return k * (3 - v) + (1 - k) * flip(v, 1)

    ya, yb = p1(y), p2(y)
    yab = p2(ya)
    sib = at(x, zh, z, y, 1 - k)
    y_peers = [at(x, zh, z, lax.rem(y + d, NY), k) for d in range(1, NY)]
    z_peers = [at(x, zh, lax.rem(z + d, NZ), y, k) for d in range(1, NZ)]
    home = flip(z, 4)
    c_peers = [
        at(lax.rem(x + d, NX), lax.rem(zh + e, 2), home, y, k)
        for d in range(NX)
        for e in range(2)
    ]
    quad = [flip(z, 1), flip(z, 2), flip(flip(z, 1), 2)]

    def along_z(d):
        to = lax.rem(zh * NZ + z + d + 2 * NZ, 2 * NZ)
        return at(x, lax.div(to, NZ), lax.rem(to, NZ), y, k)

    z_near = [along_z(d) for d in (-2, 2, -1, 1)]
    x_peers = [at(lax.rem(x + d, NX), zh, z, y, k) for d in (2, 1, 3)]
    near = z_near + x_peers + y_peers + [sib]

    def tell(sem, devices):
        for p in devices:
            pl.semaphore_signal(sem, inc=1, device_id=p, device_id_type=MESH)

    loads = {}

    def load(name, src, dst):
        cp = pltpu.make_async_copy(src, dst, ins.at[len(loads)])
        cp.start()
        loads[name] = cp

    load("qa", qa, xqa)
    load("qg", qg, xqg)
    load("pa", pa, wa)
    load("pg", pg, wg)
    barrier = pltpu.get_barrier_semaphore()
    tell(barrier, near)
    zp = lax.div(z, 2)
    for w in range(NP - 1, -1, -1):
        b = flip(zp, 2)
        for bit in (1, 2):
            b = flip(b, bit) if w & bit else b
        cols = pl.ds(pl.multiple_of(b * (2 * BLOCK), 2 * BLOCK), 2 * BLOCK)
        load(f"ta{w}", ta.at[:, cols], xa.at[w])
        load(f"tg{w}", tg.at[cols], xg.at[w])
    load("seg", seg, xseg)
    load("lr", lr, xlr)

    sends, arrivals = {}, {}

    def copy(src, dst, to, out_of, into):
        return pltpu.make_async_remote_copy(
            src_ref=src, dst_ref=dst,
            send_sem=ssem.at[sends.setdefault(out_of, len(sends))],
            recv_sem=rsem.at[arrivals.setdefault(into, len(arrivals))],
            device_id=to, device_id_type=MESH,
        )

    def send(src, dst, to, out_of, into=None):
        copy(src, dst, to, out_of, into or out_of).start()

    def arrived(ref, into):
        copy(ref, ref, sib, "c", into).wait_recv()

    def left(ref, out_of):
        copy(ref, ref, sib, out_of, "qc").wait_send()

    def project(acts, grads, store):
        a = jnp.dot(wa[...], acts, preferred_element_type=jnp.float32)
        g = lax.dot_general(
            wg[...], grads, (((1,), (1,)), ((), ())), preferred_element_type=jnp.float32
        )
        for j in range(a.shape[1] // LANES):
            store(0, j, a[:, j * LANES : (j + 1) * LANES])
            store(1, j, g[:, j * LANES : (j + 1) * LANES])

    def project_query():
        for n in ("pa", "pg", "qa", "qg"):
            loads[n].wait()

        def store(h, j, v):
            qpart[h, j] = v

        project(xqa[...], xqg[...], store)

    def project_pair(w):
        loads[f"ta{w}"].wait()
        loads[f"tg{w}"].wait()

        def store(h, j, v):
            part[w, h, j // NY, j % NY] = v

        project(xa[w], xg[w], store)

    def send_c(w):
        send(part.at[w, 1 - k], c_in.at[w], sib, "c", ("c", w))

    def own(w, i, v):
        return part[w, k, i, v] + c_in[w, i, v]

    def stage_y1(w):
        arrived(c_in.at[w], ("c", w))
        put(y1_out.at[w], [[own(w, i, ya), own(w, i, yab)] for i in range(2)])
        send(y1_out.at[w], y1_in.at[w], at(x, zh, z, ya, k), "y1", ("y1", w))

    def stage_y2(w):
        arrived(y1_in.at[w], ("y1", w))
        got = get(y1_in.at[w], 2, HALF)
        put(y2_out.at[w], [[own(w, i, yb) + got[i][1]] for i in range(2)])
        send(y2_out.at[w], y2_in.at[w], at(x, zh, z, yb, k), "y2", ("y2", w))
        for i in range(2):
            keep[w, i] = own(w, i, y) + got[i][0]

    def stage_z(w):
        arrived(y2_in.at[w], ("y2", w))
        got = get(y2_in.at[w], 2, HALF)
        for i in range(2):
            keep[w, i] = keep[w, i] + got[i][0]
        far = w // 2
        for i, q in ((1, 2), (0, 1)) if w % 2 else ((1, 0),):
            put(z_out.at[far, q], [[keep[w, lax.rem(z + i, 2)]]])
            send(
                z_out.at[far, q], z_in.at[far, q], at(x, zh, quad[q], y, k), "z", ("z", far)
            )

    def quad_sum(far):
        arrived(z_in.at[far], ("z", far))
        v = keep[2 * far, lax.rem(z, 2)]
        for q in range(3):
            v = v + get(z_in.at[far, q], 1, HALF)[0][0]
        return v

    def stage_far():
        put(f_out, [[quad_sum(1)]])
        send(f_out, f_in, at(x, zh, home, y, k), "far")

    def stage_near():
        keep[0, 0] = quad_sum(0)

    project_query()
    project_pair(3)
    pl.semaphore_wait(barrier, len(near))
    send(qpart.at[1 - k], qc_in, sib, "qc")
    send_c(3)
    tell(z_sem, z_near)
    project_pair(2)
    send_c(2)
    arrived(qc_in, "qc")
    for j in range(NY):
        v = qpart[k, j] + qc_in[j]
        qy_own[j] = v
        put(qy_out.at[j], [[v]])
    for d in (2, 1, 3):
        send(qy_out.at[lax.rem(y + d, NY)], qy_in.at[d - 1], y_peers[d - 1], "qy")
    stage_y1(3)
    project_pair(1)
    send_c(1)
    stage_y1(2)
    project_pair(0)
    send_c(0)
    stage_y1(1)
    stage_y1(0)
    arrived(qy_in, "qy")
    v = qy_own[y]
    for d in range(NY - 1):
        v = v + get(qy_in.at[d], 1, HALF)[0][0]
    pl.semaphore_wait(z_sem, len(z_near))
    tell(x_sem, x_peers)
    middle = (NZ // 2 - 1, NZ // 2)
    for h in range(2):
        qz_own[h] = v[h * QH : (h + 1) * QH]
        put(qz_out.at[h], [[v[h * QH : (h + 1) * QH]]])

    def to_middle(h):
        d = lax.rem(z - middle[h] + NZ, NZ)
        return copy(
            qz_out.at[h], qz_in.at[d], at(x, zh, middle[h], y, k), ("mid", h), "mid"
        )

    for h in range(2):

        @pl.when(z != middle[h])
        def _():
            to_middle(h).start()

    is_middle = jnp.logical_or(z == middle[0], z == middle[1])
    my_h = 1 - lax.rem(z, 2)
    arrivals["all", 0] = len(arrivals)
    arrivals["all", 1] = len(arrivals)

    def from_middle(d):
        place = qall.at[y, my_h]
        return pltpu.make_async_remote_copy(
            src_ref=place, dst_ref=place, send_sem=ssem.at[sends.setdefault("all", len(sends))],
            recv_sem=rsem.at[arrivals["all", 0] + my_h], device_id=z_peers[d - 1],
            device_id_type=MESH,
        )

    def middle_sum():
        @pl.when(is_middle)
        def _():
            arrived(qz_in.at[1:], "mid")
            total = qz_own[my_h]
            for d in range(1, NZ):
                total = total + get(qz_in.at[d], 1, QH)[0][0]
            put(qall.at[y, my_h], [[total]])
            for d in range(1, NZ):
                from_middle(d).start()

    def middle_in():
        for h in range(2):

            @pl.when(z != middle[h])
            def _():
                arrived(qall.at[y, h], ("all", h))

    stage_y2(3)
    stage_y2(2)
    stage_y2(1)
    stage_z(3)
    stage_y2(0)
    stage_z(2)
    middle_sum()
    stage_z(1)
    stage_z(0)
    stage_far()
    loads["seg"].wait()
    loads["lr"].wait()
    onehot = jnp.where(
        lax.broadcasted_iota(jnp.int32, (NQ, QTOK), 0) == xseg[...], 1.0, 0.0
    ).astype(jnp.bfloat16)
    middle_in()
    line = qall.at[y]
    for d in (2, 1, 3):
        send(line, line, y_peers[d - 1], "line")
    stage_near()
    arrived(f_in, "far")
    tok = (keep[0, 0] + get(f_in, 1, HALF)[0][0]).T
    arrived(qall.at[1:], "line")
    for j in range(NY):
        feats = jnp.concatenate([get(qall.at[j, h], 1, QH)[0][0] for h in range(2)], axis=0)
        match = jnp.dot(
            tok, feats, precision=lax.Precision.HIGHEST, preferred_element_type=jnp.float32
        )
        p_out[:, j] = match.reshape(2, ROWS, LANES)
    send(p_out.at[1 - k], p_in, sib, "pc")
    arrived(p_in, "pc")
    score = jnp.zeros((NQ, LANES), jnp.float32)
    for j in range(NY):
        prod = p_out[k, j] * p_in[j]
        high = prod.astype(jnp.bfloat16)
        rest = (prod - high.astype(jnp.float32)).astype(jnp.bfloat16)
        score += lax.dot_general(
            onehot[:, j * LANES : (j + 1) * LANES],
            jnp.concatenate([high, rest], axis=0),
            (((1,), (1,)), ((), ())), preferred_element_type=jnp.float32,
        )
    score = (xlr[0] * (score + pltpu.roll(score, ROWS, 1))).reshape(8, 8, LANES)
    low = lax.broadcasted_iota(jnp.int32, s_out.shape, 2) < ROWS
    s_out[...] = jnp.where(low, score[:, :4], score[:, 4:])
    pl.semaphore_wait(x_sem, len(x_peers))
    for i, p in enumerate(c_peers):
        send(s_out.at[p[0]], s_in.at[i], p, "fin")
    arrived(s_in, "fin")
    total = s_in[0]
    for i in range(1, len(c_peers)):
        total = total + s_in[i]
    out[0:4] = total[:, :ROWS]
    out[4:8] = total[:, ROWS:]
    for ref, out_of in (
        (qc_in, "qc"), (c_in, "c"), (qy_in, "qy"), (y1_in, "y1"), (y2_in, "y2"), (z_in, "z"),
        (f_in, "far"), (qall.at[1:], "line"), (p_in, "pc"), (s_in, "fin"),
    ):
        left(ref, out_of)
    for h in range(2):

        @pl.when(z != middle[h])
        def _():
            left(qz_out.at[h], ("mid", h))

    @pl.when(is_middle)
    def _():
        left(qz_in.at[1:], "all")


def body(
    train_acts, train_grads, query_acts, query_grads, query_segment, proj_act, proj_grad, lrates
):
    ff, d = train_acts.shape[2], train_grads.shape[2]
    f32, bf16, i32 = jnp.float32, jnp.bfloat16, jnp.int32
    vmem = pltpu.VMEM
    hbm = pl.BlockSpec(memory_space=pltpu.HBM)
    res = pl.pallas_call(
        kernel,
        out_shape=jax.ShapeDtypeStruct((8, ROWS), f32),
        in_specs=[hbm] * 8,
        out_specs=pl.BlockSpec(memory_space=pltpu.VMEM),
        scratch_shapes=[
            vmem((NP, ff, 2 * BLOCK), bf16),
            vmem((NP, 2 * BLOCK, d), bf16),
            vmem((ff, QTOK), bf16),
            vmem((QTOK, d), bf16),
            vmem((1, QTOK), i32),
            vmem((HALF, ff), bf16),
            vmem((HALF, d), bf16),
            pltpu.SMEM((1,), f32),
            pltpu.SemaphoreType.DMA((2 * NP + 6,)),
            vmem((NP, 2, 2, NY, HALF, LANES), f32),
            vmem((NP, 2, NY, HALF, LANES), f32),
            vmem((NP, 2 * HALF + 2, LANES), i32),
            vmem((NP, 2 * HALF + 2, LANES), i32),
            vmem((NP, HALF + 2, LANES), i32),
            vmem((NP, HALF + 2, LANES), i32),
            vmem((2, 3, QH + 1, LANES), i32),
            vmem((2, 3, QH + 1, LANES), i32),
            vmem((QH + 1, LANES), i32),
            vmem((QH + 1, LANES), i32),
            vmem((NP, 2, HALF, LANES), f32),
            vmem((2, NY, HALF, LANES), f32),
            vmem((NY, HALF, LANES), f32),
            vmem((NY, HALF, LANES), f32),
            vmem((NY, QH + 1, LANES), i32),
            vmem((NY - 1, QH + 1, LANES), i32),
            vmem((2, QH, LANES), f32),
            vmem((2, QH // 2 + 1, LANES), i32),
            vmem((NZ, QH // 2 + 1, LANES), i32),
            vmem((NY, 2, QH // 2 + 1, LANES), i32),
            vmem((2, NY, ROWS, LANES), f32),
            vmem((NY, ROWS, LANES), f32),
            vmem((8, 4, LANES), f32),
            vmem((8, 4, LANES), f32),
            pltpu.SemaphoreType.DMA((13,)),
            pltpu.SemaphoreType.DMA((25,)),
            pltpu.SemaphoreType.REGULAR,
            pltpu.SemaphoreType.REGULAR,
        ],
        compiler_params=pltpu.CompilerParams(
            collective_id=0, has_side_effects=True, vmem_limit_bytes=60 << 20
        ),
        name="tracin",
    )(
        train_acts[0].T,
        train_grads[0],
        query_acts[0].T,
        query_grads[0],
        query_segment.reshape(1, QTOK),
        proj_act.T,
        proj_grad.T,
        lrates,
    )
    return res.T


def solution(mesh):
    placed = (
        P("ckpt", None, "unit"),
        P("ckpt", None, "unit"),
        P("ckpt", None, "unit"),
        P("ckpt", None, "unit"),
        P(),
        P("unit", None),
        P("unit", None),
        P("ckpt"),
    )
    return jax.shard_map(
        body, mesh=mesh, in_specs=placed, out_specs=P("unit", "ckpt"), check_vma=False
    )
```

time: 48.1 us -> 41.6 us (0.86)
  Pallas kernels: 46 us -> 39.5 us
    pallas_call x1, Pallas kernels: 46 us -> 39.5 us  [body(): pl.pallas_call(kernel, out_shape=jax.ShapeDtypeStruct((8, ROWS), f32), in...]
where the time goes in v3:
time: 41.6 us; the launch traced here: 41.4 us
  Pallas kernels  39.5 us (95%)
  local copies, waits for them, and re-layouts  1.28 us (3%)
  between operations  0.66 us (2%)
    pallas_call x1, Pallas kernels, body(): pl.pallas_call(kernel, out_shape=jax.ShapeDtypeStruct((8, ROWS), f32), in...  39.5 us
    unnamed x1, local copies, waits for them, and re-layouts  1.28 us

profile of v3, /device:TPU:1, one launch (start us, length us, event | category | flops | bytes accessed | tf_op | source)
XLA Modules:
  0.0 41.4 jit_solution(11223794732645254786)
XLA Ops:
  0.7 39.5 %tracin.1 = f32[8,64]{1,0:T(8,128)} custom-call(bf16[344,4096]{1,0:T(8,128)(2,1)} %bitcast.12, bf16[4096,128]{1,0:T(8,128)(2,1)} %bitcast.13, bf16[344,512]{1,0:T(8,128)(2,1)} %bitcast.14, bf16[512,128]{1,0:T(8,128)(2,1)} %bitcast.15, s32[1,512]{1,0:T(1,128)} %bitcast.19, bf16[64,344]{1,0:T(8,128)(2,1)} %bitcast.16, bf16[64,128]{1,0:T(8,128)(2,1)} %bitcast.17, ...), custom_call_target="tpu_custom_call" | custom-call | tf_op jit(solution)/shard_map/tracin/pallas_call | solution.py:373
  40.1 1.3 %copy.11 = f32[64,8]{0,1:T(8,128)} copy(f32[64,8]{0,1:T(8,128)} %bitcast.18) | data formatting | bytes 4096

commit v4 on v3

--- a/solution.py
+++ b/solution.py
@@ -56,9 +56,14 @@
     return found
 
 
+def terms(v):
+    high = v.astype(jnp.bfloat16).astype(jnp.float32)
+    return high, (v - high).astype(jnp.bfloat16).astype(jnp.float32)
+
+
 def kernel(
     ta, tg, qa, qg, seg, pa, pg, lr, out,
-    xa, xg, xqa, xqg, xseg, wa, wg, xlr, ins,
+    xa, xg, xqa, xqg, xseg, wa, wg, ins,
     part, c_in, y1_out, y1_in, y2_out, y2_in, z_out, z_in, f_out, f_in, keep,
     qpart, qc_in, qy_own, qy_out, qy_in, qz_own, qz_out, qz_in, qall, p_out, p_in, s_out, s_in,
     ssem, rsem, z_sem, x_sem,
@@ -85,7 +90,7 @@
     home = flip(z, 4)
     c_peers = [
         at(lax.rem(x + d, NX), lax.rem(zh + e, 2), home, y, k)
-        for d in range(NX)
+        for d in (0, 2, 1, 3)
         for e in range(2)
     ]
     quad = [flip(z, 1), flip(z, 2), flip(flip(z, 1), 2)]
@@ -124,7 +129,6 @@
         load(f"ta{w}", ta.at[:, cols], xa.at[w])
         load(f"tg{w}", tg.at[cols], xg.at[w])
     load("seg", seg, xseg)
-    load("lr", lr, xlr)
 
     sends, arrivals = {}, {}
 
@@ -287,12 +291,16 @@
             for d in range(1, NZ):
                 from_middle(d).start()
 
-    def middle_in():
-        for h in range(2):
-
-            @pl.when(z != middle[h])
-            def _():
-                arrived(qall.at[y, h], ("all", h))
+    def middle_in(h):
+        @pl.when(z != middle[0] + h)
+        def _():
+            pltpu.make_async_remote_copy(
+                src_ref=qall.at[y, h], dst_ref=qall.at[y, h], send_sem=ssem.at[0],
+                recv_sem=rsem.at[arrivals["all", 0] + h], device_id=sib, device_id_type=MESH,
+            ).wait_recv()
+
+        for d in (2, 1, 3):
+            send(qall.at[y, h], qall.at[y, h], y_peers[d - 1], "line")
 
     stage_y2(3)
     stage_y2(2)
@@ -301,45 +309,46 @@
     stage_y2(0)
     stage_z(2)
     middle_sum()
+    stage_far()
     stage_z(1)
     stage_z(0)
-    stage_far()
     loads["seg"].wait()
-    loads["lr"].wait()
     onehot = jnp.where(
         lax.broadcasted_iota(jnp.int32, (NQ, QTOK), 0) == xseg[...], 1.0, 0.0
     ).astype(jnp.bfloat16)
-    middle_in()
-    line = qall.at[y]
-    for d in (2, 1, 3):
-        send(line, line, y_peers[d - 1], "line")
+    first_h = lax.div(z, NZ // 2)
+    middle_in(first_h)
+    middle_in(1 - first_h)
     stage_near()
     arrived(f_in, "far")
-    tok = (keep[0, 0] + get(f_in, 1, HALF)[0][0]).T
+    tok = keep[0, 0] + get(f_in, 1, HALF)[0][0]
+    high, rest = terms(tok)
+    lhs = jnp.concatenate([high, high, rest], axis=0).T.astype(jnp.bfloat16)
     arrived(qall.at[1:], "line")
+    rhs = []
     for j in range(NY):
         feats = jnp.concatenate([get(qall.at[j, h], 1, QH)[0][0] for h in range(2)], axis=0)
-        match = jnp.dot(
-            tok, feats, precision=lax.Precision.HIGHEST, preferred_element_type=jnp.float32
-        )
-        p_out[:, j] = match.reshape(2, ROWS, LANES)
+        high, rest = terms(feats)
+        rhs.append(jnp.concatenate([high, rest, high], axis=0).astype(jnp.bfloat16))
+    match = jnp.dot(lhs, jnp.concatenate(rhs, axis=1), preferred_element_type=jnp.float32)
+    for j in range(NY):
+        p_out[:, j] = match[:, j * LANES : (j + 1) * LANES].reshape(2, ROWS, LANES)
     send(p_out.at[1 - k], p_in, sib, "pc")
     arrived(p_in, "pc")
     score = jnp.zeros((NQ, LANES), jnp.float32)
     for j in range(NY):
         prod = p_out[k, j] * p_in[j]
-        high = prod.astype(jnp.bfloat16)
-        rest = (prod - high.astype(jnp.float32)).astype(jnp.bfloat16)
+        high, rest = terms(prod)
         score += lax.dot_general(
             onehot[:, j * LANES : (j + 1) * LANES],
-            jnp.concatenate([high, rest], axis=0),
+            jnp.concatenate([high, rest], axis=0).astype(jnp.bfloat16),
             (((1,), (1,)), ((), ())), preferred_element_type=jnp.float32,
         )
-    score = (xlr[0] * (score + pltpu.roll(score, ROWS, 1))).reshape(8, 8, LANES)
+    score = (lr[0] * (score + pltpu.roll(score, ROWS, 1))).reshape(8, 8, LANES)
     low = lax.broadcasted_iota(jnp.int32, s_out.shape, 2) < ROWS
     s_out[...] = jnp.where(low, score[:, :4], score[:, 4:])
     pl.semaphore_wait(x_sem, len(x_peers))
-    for i, p in enumerate(c_peers):
+    for i, p in list(enumerate(c_peers))[2:] + list(enumerate(c_peers))[:2]:
         send(s_out.at[p[0]], s_in.at[i], p, "fin")
     arrived(s_in, "fin")
     total = s_in[0]
@@ -372,8 +381,8 @@
     hbm = pl.BlockSpec(memory_space=pltpu.HBM)
     res = pl.pallas_call(
         kernel,
-        out_shape=jax.ShapeDtypeStruct((8, ROWS), f32),
-        in_specs=[hbm] * 8,
+        out_shape=pltpu.VMEM((8, ROWS), f32),
+        in_specs=[hbm] * 7 + [pl.BlockSpec(memory_space=pltpu.SMEM)],
         out_specs=pl.BlockSpec(memory_space=pltpu.VMEM),
         scratch_shapes=[
             vmem((NP, ff, 2 * BLOCK), bf16),
@@ -383,8 +392,7 @@
             vmem((1, QTOK), i32),
             vmem((HALF, ff), bf16),
             vmem((HALF, d), bf16),
-            pltpu.SMEM((1,), f32),
-            pltpu.SemaphoreType.DMA((2 * NP + 6,)),
+            pltpu.SemaphoreType.DMA((2 * NP + 5,)),
             vmem((NP, 2, 2, NY, HALF, LANES), f32),
             vmem((NP, 2, NY, HALF, LANES), f32),
             vmem((NP, 2 * HALF + 2, LANES), i32),
@@ -415,17 +423,22 @@
             pltpu.SemaphoreType.REGULAR,
         ],
         compiler_params=pltpu.CompilerParams(
-            collective_id=0, has_side_effects=True, vmem_limit_bytes=60 << 20
+            collective_id=0, has_side_effects=True, vmem_limit_bytes=48 << 20
         ),
         name="tracin",
     )(
-        train_acts[0].T,
-        train_grads[0],
-        query_acts[0].T,
-        query_grads[0],
-        query_segment.reshape(1, QTOK),
-        proj_act.T,
-        proj_grad.T,
+        *(
+            pltpu.with_memory_space_constraint(v, pltpu.HBM)
+            for v in (
+                train_acts[0].T,
+                train_grads[0],
+                query_acts[0].T,
+                query_grads[0],
+                query_segment.reshape(1, QTOK),
+                proj_act.T,
+                proj_grad.T,
+            )
+        ),
         lrates,
     )
     return res.T

time: 41.6 us -> 40.2 us (0.966)
  Pallas kernels: 39.5 us -> 38.8 us
  local copies, waits for them, and re-layouts: 1.28 us -> 0.6 us
    pallas_call x1, Pallas kernels: 39.5 us -> 38.8 us  [body(): pl.pallas_call(kernel, out_shape=pltpu.VMEM((8, ROWS), f32), in_specs=[hb...]
    unnamed x1, local copies, waits for them, and re-layouts: 1.28 us -> 0.6 us
where the time goes in v4:
time: 40.2 us; the launch traced here: 40 us
  Pallas kernels  38.8 us (97%)
  between operations  0.66 us (2%)
  local copies, waits for them, and re-layouts  0.6 us (1%)
    pallas_call x1, Pallas kernels, body(): pl.pallas_call(kernel, out_shape=pltpu.VMEM((8, ROWS), f32), in_specs=[hb...  38.8 us

profile of v4, /device:TPU:1, one launch (start us, length us, event | category | flops | bytes accessed | tf_op | source)
XLA Modules:
  0.0 40.0 jit_solution(15105954918313472999)
XLA Ops:
  0.7 38.8 %tracin.1 = f32[8,64]{1,0:T(8,128)S(1)} custom-call(bf16[344,4096]{1,0:T(8,128)(2,1)} %bitcast.13, bf16[4096,128]{1,0:T(8,128)(2,1)} %bitcast.14, bf16[344,512]{1,0:T(8,128)(2,1)} %bitcast.15, bf16[512,128]{1,0:T(8,128)(2,1)} %bitcast.16, s32[1,512]{1,0:T(1,128)} %bitcast.19, bf16[64,344]{1,0:T(8,128)(2,1)} %bitcast.17, bf16[64,128]{1,0:T(8,128)(2,1)} %bitcast.18, ...), custom_call_target="tpu_custom_call" | custom-call | tf_op jit(solution)/shard_map/tracin/pallas_call | solution.py:382
  39.4 0.6 %copy.10 = f32[64,8]{0,1:T(8,128)} copy(f32[64,8]{0,1:T(8,128)S(1)} %bitcast.12) | data formatting | bytes 4096

commit v5 on v4

--- a/solution.py
+++ b/solution.py
@@ -121,14 +121,16 @@
     barrier = pltpu.get_barrier_semaphore()
     tell(barrier, near)
     zp = lax.div(z, 2)
-    for w in range(NP - 1, -1, -1):
+
+    def load_pair(w):
         b = flip(zp, 2)
         for bit in (1, 2):
             b = flip(b, bit) if w & bit else b
         cols = pl.ds(pl.multiple_of(b * (2 * BLOCK), 2 * BLOCK), 2 * BLOCK)
         load(f"ta{w}", ta.at[:, cols], xa.at[w])
         load(f"tg{w}", tg.at[cols], xg.at[w])
-    load("seg", seg, xseg)
+
+    load_pair(3)
 
     sends, arrivals = {}, {}
 
@@ -158,9 +160,10 @@
             store(0, j, a[:, j * LANES : (j + 1) * LANES])
             store(1, j, g[:, j * LANES : (j + 1) * LANES])
 
-    def project_query():
+    def project_query(then):
         for n in ("pa", "pg", "qa", "qg"):
             loads[n].wait()
+        then()
 
         def store(h, j, v):
             qpart[h, j] = v
@@ -221,14 +224,18 @@
     def stage_near():
         keep[0, 0] = quad_sum(0)
 
-    project_query()
-    project_pair(3)
+    project_query(lambda: [load_pair(w) for w in (2, 1, 0)] + [load("seg", seg, xseg)])
     pl.semaphore_wait(barrier, len(near))
     send(qpart.at[1 - k], qc_in, sib, "qc")
+    project_pair(3)
     send_c(3)
     tell(z_sem, z_near)
-    project_pair(2)
-    send_c(2)
+
+    @pl.when(k == 1)
+    def _():
+        project_pair(2)
+        send_c(2)
+
     arrived(qc_in, "qc")
     for j in range(NY):
         v = qpart[k, j] + qc_in[j]
@@ -236,6 +243,12 @@
         put(qy_out.at[j], [[v]])
     for d in (2, 1, 3):
         send(qy_out.at[lax.rem(y + d, NY)], qy_in.at[d - 1], y_peers[d - 1], "qy")
+
+    @pl.when(k == 0)
+    def _():
+        project_pair(2)
+        send_c(2)
+
     stage_y1(3)
     project_pair(1)
     send_c(1)

time: 40.2 us -> 40 us (level)
  no operation moved by 1% of the time
where the time goes in v5:
time: 40 us; the launch traced here: 39.8 us
  Pallas kernels  38.6 us (96%)
  between operations  0.66 us (2%)
  local copies, waits for them, and re-layouts  0.6 us (2%)
    pallas_call x1, Pallas kernels, body(): pl.pallas_call(kernel, out_shape=pltpu.VMEM((8, ROWS), f32), in_specs=[hb...  38.6 us

profile of v5, /device:TPU:1, one launch (start us, length us, event | category | flops | bytes accessed | tf_op | source)
XLA Modules:
  0.0 39.8 jit_solution(799213641241942789)
XLA Ops:
  0.7 38.6 %tracin.1 = f32[8,64]{1,0:T(8,128)S(1)} custom-call(bf16[344,4096]{1,0:T(8,128)(2,1)} %bitcast.13, bf16[4096,128]{1,0:T(8,128)(2,1)} %bitcast.14, bf16[344,512]{1,0:T(8,128)(2,1)} %bitcast.15, bf16[512,128]{1,0:T(8,128)(2,1)} %bitcast.16, s32[1,512]{1,0:T(1,128)} %bitcast.19, bf16[64,344]{1,0:T(8,128)(2,1)} %bitcast.17, bf16[64,128]{1,0:T(8,128)(2,1)} %bitcast.18, ...), custom_call_target="tpu_custom_call" | custom-call | tf_op jit(solution)/shard_map/tracin/pallas_call | solution.py:395
  39.2 0.6 %copy.10 = f32[64,8]{0,1:T(8,128)} copy(f32[64,8]{0,1:T(8,128)S(1)} %bitcast.12) | data formatting | bytes 4096

commit v6 on v5

--- a/solution.py
+++ b/solution.py
@@ -233,8 +233,9 @@
 
     @pl.when(k == 1)
     def _():
-        project_pair(2)
-        send_c(2)
+        for w in (2, 1):
+            project_pair(w)
+            send_c(w)
 
     arrived(qc_in, "qc")
     for j in range(NY):
@@ -250,8 +251,12 @@
         send_c(2)
 
     stage_y1(3)
-    project_pair(1)
-    send_c(1)
+
+    @pl.when(k == 0)
+    def _():
+        project_pair(1)
+        send_c(1)
+
     stage_y1(2)
     project_pair(0)
     send_c(0)

time: 40 us -> 40 us (level)
  no operation moved by 1% of the time
where the time goes in v6:
time: 40 us; the launch traced here: 39.8 us
  Pallas kernels  38.6 us (96%)
  between operations  0.66 us (2%)
  local copies, waits for them, and re-layouts  0.6 us (2%)
    pallas_call x1, Pallas kernels, body(): pl.pallas_call(kernel, out_shape=pltpu.VMEM((8, ROWS), f32), in_specs=[hb...  38.6 us

profile of v6, /device:TPU:1, one launch (start us, length us, event | category | flops | bytes accessed | tf_op | source)
XLA Modules:
  0.0 39.8 jit_solution(2242857020977303058)
XLA Ops:
  0.7 38.6 %tracin.1 = f32[8,64]{1,0:T(8,128)S(1)} custom-call(bf16[344,4096]{1,0:T(8,128)(2,1)} %bitcast.13, bf16[4096,128]{1,0:T(8,128)(2,1)} %bitcast.14, bf16[344,512]{1,0:T(8,128)(2,1)} %bitcast.15, bf16[512,128]{1,0:T(8,128)(2,1)} %bitcast.16, s32[1,512]{1,0:T(1,128)} %bitcast.19, bf16[64,344]{1,0:T(8,128)(2,1)} %bitcast.17, bf16[64,128]{1,0:T(8,128)(2,1)} %bitcast.18, ...), custom_call_target="tpu_custom_call" | custom-call | tf_op jit(solution)/shard_map/tracin/pallas_call | solution.py:400
  39.2 0.6 %copy.10 = f32[64,8]{0,1:T(8,128)} copy(f32[64,8]{0,1:T(8,128)S(1)} %bitcast.12) | data formatting | bytes 4096
